TPU v7x, 128 devices: a whole 4x4x4 slice. The times are simulated.
128 devices in a mesh: region: 4 (over x_lo, core), subj: 32 (over y, z, x_hi).
Axes of the slice: x: 4 (x_hi: 2, x_lo: 2; x = x_hi * 2 + x_lo), y: 4, z: 4, core: 2. Of those that a mesh axis runs over, the one named last changes fastest.
Arguments:
- coords: float32 [8192, 3, 2048], P('subj', None, 'region'), may hold values from -30 to 30
- transform: float32 [8192, 3, 3], P('subj'), may hold values from -3.5 to 3.5
- labels: int32 [2048, 1], P('region'), may hold values from 0 to 3; in each aligned block of 512 rows (0 to 511, 512 to 1023, ...) at most 256 rows name the same one
- subject_order: int32 [8192], replicated, may hold values from 0 to 8191, each once
Outputs:
- region_gram: float32 [4, 8192, 8192], P('region', 'subj')
Inputs may be any that keep to these rules, and one draw needn't show every extreme that they name: `labels`: among the 512 vertices of one device no region label occurs more than 256 times, and some label reaches 256. `subject_order`: a permutation of the subjects.
All inputs are finite; a program needn't handle non-finite values.
Results may differ from a plain program's by a relative error of at most 0.0012.
Values may be sent and summed in bfloat16 or wider, within the bound.
A program may use at most 128 MiB of HBM per device.

v0:
```python
import jax
import jax.numpy as jnp
from jax import lax
from jax.sharding import PartitionSpec as P

CAP = 256


def tile_block(left, right):
    return jnp.einsum("acgv,bcgv->gab", left, right, preferred_element_type=jnp.float32)


def local(coords, transform, labels, subject_order):
    per_dev = coords.shape[0]
    local_verts = coords.shape[2]
    regions_count = lax.axis_size("region")
    verts_total = local_verts * regions_count
    moved = (
        transform[:, :, 0:1] * coords[:, 0:1, :]
        + transform[:, :, 1:2] * coords[:, 1:2, :]
        + transform[:, :, 2:3] * coords[:, 2:3, :]
    )
    totals = lax.psum(jnp.sum(moved, axis=2), "region")
    centered = (moved - (totals / verts_total)[:, :, None]).astype(jnp.bfloat16)
    label_row = labels[:, 0]
    onehot = (label_row[None, :] == jnp.arange(regions_count, dtype=jnp.int32)[:, None]).astype(
        jnp.int32
    )
    ranks = jnp.sum((jnp.cumsum(onehot, axis=1) - 1) * onehot, axis=0)
    target = label_row * CAP + ranks
    buckets = (
        jnp.zeros((per_dev, 3, regions_count * CAP), jnp.bfloat16).at[:, :, target].set(centered)
    )
    buckets = buckets.reshape(per_dev, 3, regions_count, CAP)
    received = lax.all_to_all(buckets, "region", split_axis=2, concat_axis=2, tiled=True)
    panel = received.reshape(per_dev, 3, 1, regions_count * CAP)
    gram_rows = tile_block(panel, lax.all_gather(panel, "subj", axis=0, tiled=True))
    gram_rows = gram_rows * (1.0 / (3.0 * verts_total))
    return jnp.take(gram_rows, subject_order, axis=2)


def solution(mesh):
    placed = (P("subj", None, "region"), P("subj", None, None), P("region", None), P())
    return jax.shard_map(
        local, mesh=mesh, in_specs=placed, out_specs=P("region", "subj", None), check_vma=False
    )
```

profile of v0, /device:TPU:3, one launch (start us, length us, event | category | flops | bytes accessed | tf_op | source)
XLA Modules:
  0.0 525.8 jit_solution(15208422235316502730)
XLA Ops:
  6.5 0.8 fusion.12
  7.4 1.5 slice_bitcast_fusion.2
  8.9 0.2 copy.17
  9.1 0.2 copy.18
  9.3 0.2 copy.19
  9.5 1.1 fusion.8
  10.6 5.7 %psum.7 = f32[256,3]{0,1:T(4,128)S(1)} all-reduce(f32[256,3]{0,1:T(4,128)S(1)} %fusion.8), channel_id=1, replica_groups=mesh['region'=4,'subj'=32] {'region'}, use_global_device_ids=true, to_apply=%region_4.5 | all-reduce | flops 768 | bytes 6144 | tf_op jit(solution)/shard_map/psum | solution.py:23
  16.4 1.0 fusion.9
  17.4 1.2 reduce-window.6
  18.6 0.2 slice_reduce_fusion
  18.8 0.2 reduce-window.9
  19.1 0.5 broadcast_in_dim.19
  19.7 13.6 %scatter_fusion = bf16[256,3,1024]{0,1,2:T(4,128)(2,1)S(1)} fusion(bf16[256,3,1024]{0,1,2:T(4,128)(2,1)S(1)} %broadcast_in_dim.19, s32[512]{0:T(512)S(1)} %bitcast.49, bf16[512,256,3]{1,2,0:T(4,128)(2,1)S(1)} %fusion.9), kind=kCustom, calls=%fused_computation.1 | custom fusion | bytes 2361344 | tf_op jit(solution)/shard_map/scatter | solution.py:32
  33.2 2.4 copy.20
  35.6 23.7 %all_to_all.5 = bf16[256,3,4,256]{3,0,1,2:T(8,128)(2,1)S(1)} all-to-all(bf16[256,3,4,256]{3,0,1,2:T(8,128)(2,1)} %copy.20), channel_id=1, replica_groups=mesh['region'=4,'subj'=32] {'region'}, dimensions={2} | all-to-all | bytes 3145728 | tf_op jit(solution)/shard_map/all_to_all | solution.py:35
  59.3 1.2 copy.21
  60.5 2.3 reshape.82
  62.9 0.2 copy.28
  63.1 371.1 %all-gather.2.cloned.1.call-done = bf16[8192,3,1,1024]{3,0,1,2:T(8,128)(2,1)} async-done(((bf16[256,3,1,1024]{3,0,1,2:T(8,128)(2,1)}), bf16[8192,3,1,1024]{3,0,1,2:T(8,128)(2,1)}) %all-gather.2.cloned.1.call-update) | async-done | bytes 50331664 | tf_op jit(solution)/shard_map/all_gather | solution.py:37
  434.3 24.5 %fusion.5 = f32[256,8192]{1,0:T(8,128)} fusion(bf16[256,3,1024]{2,0,1:T(8,128)(2,1)S(1)} %bitcast.42, bf16[8192,3,1,1024]{3,0,1,2:T(8,128)(2,1)} %all-gather.2.cloned.1.call-done), kind=kOutput, calls=%fused_computation.5 | convolution fusion | flops 12886999040 | bytes 60293120 | tf_op jit(solution)/shard_map/acgv,bcgv->gab/dot_general | solution.py:10
  458.8 9.0 %copy.23 = f32[256,8192]{0,1:T(8,128)} copy(f32[256,8192]{1,0:T(8,128)} %fusion.5) | data formatting | bytes 16777216 | tf_op jit(solution)/shard_map/mul | solution.py:38
  467.8 34.9 %gather_fusion = f32[8192,256]{1,0:T(8,128)} fusion(f32[256,8192]{0,1:T(8,128)} %copy.23, s32[8192]{0:T(1024)S(1)} %fusion.10), kind=kCustom, calls=%fused_computation | custom fusion | bytes 16809984 | tf_op jit(solution)/shard_map/jit(_take)/gather | solution.py:39
  502.7 7.4 %bitcast_select_fusion = f32[1,256,8192]{1,2,0:T(8,128)} fusion(f32[8192,256]{1,0:T(8,128)} %gather_fusion, pred[8192]{0:T(1024)(128)(4,1)S(1)} %compare_and_fusion), kind=kLoop, calls=%fused_computation.6 | loop fusion | flops 2097152 | bytes 16785408 | tf_op jit(solution)/shard_map/jit(_take)/select_n | solution.py:39
  510.1 8.9 %copy.24 = f32[1,256,8192]{2,1,0:T(8,128)} copy(f32[1,256,8192]{1,2,0:T(8,128)} %bitcast_select_fusion) | data formatting | bytes 16777216 | tf_op jit(solution)/shard_map/jit(_take)/select_n | solution.py:39
  (14 shorter events, 0.2 us)
Async XLA Ops:
  6.5 427.7 %all-gather.2.cloned.1.call-start = ((), (), s32[]{:S(2)}) async-start(), calls=%async_computation.1 | async-start | bytes 51904512 | tf_op jit(solution)/shard_map/all_gather | solution.py:37
  9.5 7.9 %copy-start.1 = (s32[512,1]{0,1:T(1,128)S(1)}, s32[512,1]{0,1:T(1,128)}, u32[]{:S(2)}) copy-start(s32[512,1]{0,1:T(1,128)} %param.6) | copy-start | bytes 6148
  60.5 2.4 copy-start
Sparse Core Ops, SparseCore 0:
  63.0 371.2 all-gather.1
where the time goes:
time: 528 us; the launch traced here: 526 us
  waiting for transfers between devices  371 us (70%)
  local copies, waits for them, and re-layouts  76.1 us (14%)
  blocking collectives  29.4 us (6%)
  matrix products  24.5 us (5%)
  between operations  13.5 us (3%)
  other arithmetic  11.1 us (2%)
    all_gather x1, waiting for transfers between devices, local(): lax.all_gather(panel, 'subj', axis=0, tiled=True)  371 us
    gather x1, local copies, waits for them, and re-layouts, local(): return jnp.take(gram_rows, subject_order, axis=2)  34.9 us
    dot_general x1, matrix products, tile_block(): jnp.einsum('acgv,bcgv->gab', left, right, preferred_element_type=jnp.floa...  24.5 us
    all_to_all x1, blocking collectives, local(): lax.all_to_all(buckets, 'region', split_axis=2, concat_axis=2, tiled=True)  23.7 us
    scatter x1, local copies, waits for them, and re-layouts, local(): jnp.zeros((per_dev, 3, regions_count * CAP), jnp.bfloat16).at[:, :, target]  13.6 us
  transfers between devices with their start and end apart: 1, of which 1 were waited for; matrix products, arithmetic and copies ran while one was open for 0% of the time, Pallas kernels for 0%

commit v1 on v0

v1 whole, which is shorter than its diff:
```python
import functools

import jax
import jax.numpy as jnp
from jax import lax
from jax.experimental import pallas as pl
from jax.experimental.pallas import tpu as pltpu
from jax.sharding import PartitionSpec as P

CAP = 256
B = 256
G = 4
F = 3 * CAP
MESH = pl.DeviceIdType.MESH
NT = (((1,), (1,)), ((), ()))


def dev(l, c, y, z, u):
    return (2 * l + c, 8 * lax.rem(y, 4) + 2 * lax.rem(z, 4) + u)


def gram_kernel(cent, tgt, out, snd, panels, res, relay_ss, relay_rs, ring_ss, ring_rs, sib_ss, sib_rs, res_ss, res_rs):
    r, s = lax.axis_index("region"), lax.axis_index("subj")
    l, c = r // 2, lax.rem(r, 2)
    y, z, u = s // 8, lax.rem(s // 2, 4), lax.rem(s, 2)
    barrier = pltpu.get_barrier_semaphore()
    own = c == u

    def copy(src, dst, ss, rs, to):
        return pltpu.make_async_remote_copy(
            src_ref=src, dst_ref=dst, send_sem=ss, recv_sem=rs, device_id=to, device_id_type=MESH
        )

    for k in range(1, 8):
        q = lax.rem(l * 4 + c * 2 + u + k, 8)
        pl.semaphore_signal(barrier, inc=1, device_id=dev(q // 4, lax.rem(q // 2, 2), y, z, lax.rem(q, 2)), device_id_type=MESH)
    for k in range(1, 4):
        for cc in range(2):
            for uu in range(2):
                pl.semaphore_signal(barrier, inc=1, device_id=dev(l, cc, y + k, z, uu), device_id_type=MESH)
                pl.semaphore_signal(barrier, inc=1, device_id=dev(l, cc, y, z + k, uu), device_id_type=MESH)
    pl.semaphore_wait(barrier, 31)

    row = tgt[0:1, :]
    for region in range(G):
        lr, ur = region // 2, region % 2
        slots = lax.broadcasted_iota(jnp.int32, (CAP, row.shape[1]), 0) + region * CAP
        pick = jnp.where(slots == row, 1.0, 0.0).astype(jnp.bfloat16)
        for d in range(3):
            snd[region, :, d * CAP : (d + 1) * CAP] = lax.dot_general(
                cent[d], pick, NT, preferred_element_type=jnp.float32
            ).astype(jnp.bfloat16)
        mine = jnp.logical_and(own, jnp.logical_and(l == lr, u == ur))

        @pl.when(mine)
        def _():
            pltpu.make_async_copy(snd.at[region], panels.at[0, r], relay_rs.at[r]).start()

        @pl.when(jnp.logical_not(mine))
        def _():
            copy(snd.at[region], panels.at[0, r], relay_ss.at[region], relay_rs.at[r], dev(lr, u, y, z, ur)).start()

    sibling = dev(l, 1 - c, y, z, u)
    yp, ym = dev(l, c, y + 1, z, u), dev(l, c, y + 3, z, u)
    zp, zm = dev(l, c, y, z + 1, u), dev(l, c, y, z + 3, u)

    def send(kind, src, dst, g, to):
        return copy(panels.at[src, g], panels.at[dst, g], ring_ss.at[kind, g], ring_rs.at[kind, g], to)

    def share(slot, g):
        return copy(panels.at[2 * slot, g], panels.at[2 * slot + 1, g], sib_ss.at[slot, g], sib_rs.at[slot, g], sibling)

    for g in range(G):
        copy(snd.at[0], panels.at[0, g], relay_ss.at[0], relay_rs.at[g], sibling).wait_recv()
        send(0, 0, 6, g, yp).start()
        send(1, 0, 2, g, ym).start()
        send(2, 0, 10, g, zp).start()
        send(3, 0, 8, g, zm).start()
        share(0, g).start()

    def block(bi, ai, rows=B, at=0):
        total = None
        for g in range(G):
            part = lax.dot_general(
                panels[bi, g, at : at + rows, :], panels[ai, g], NT, preferred_element_type=jnp.float32
            )
            total = part if total is None else total + part
        return total * (1.0 / (3.0 * 2048))

    def number(yb, zb, hb):
        return 8 * lax.rem(yb, 4) + 2 * lax.rem(zb, 4) + hb

    sent = []

    def deliver(t, bi, ai, b, owner, maybe_self=False, half=None):
        if half is None:
            res[t] = block(bi, ai)
            src, dst, sem = res.at[t], out.at[b], res_rs.at[b]
        else:
            part = pl.ds(half * 128, 128)
            res[t, part, :] = block(bi, ai, 128, half * 128)
            src, dst = res.at[t, part], out.at[b, part]
            sem = res_rs.at[b] if half == 0 else res_rs.at[32 + lax.rem(b, 2)]
        remote = copy(src, dst, res_ss.at[t], sem, owner)
        if maybe_self:

            @pl.when(own)
            def _():
                pltpu.make_async_copy(src, dst, sem).start()

            @pl.when(jnp.logical_not(own))
            def _():
                remote.start()
        else:
            remote.start()
        sent.append((remote, maybe_self))

    def cols(dz):
        return 0 if dz == 0 else 7 + dz

    def head(j):
        return c if j == 0 else 1 - c

    def home_rows(t, dz):
        for j in range(2):
            deliver(t + j, cols(dz), j, number(y, z + dz, c), dev(l, u, y, z, head(j)), maybe_self=j == 0)

    def home_cols(t, dy):
        for j in range(2):
            deliver(t + j, 2 * dy + j, 0, number(y + dy, z, head(j)), dev(l, u, y, z, c), maybe_self=True)

    def by_y(t, dy, dz, half=None):
        for j in range(2):
            deliver(t + j, cols(dz), 2 * dy + j, number(y, z + dz, c), dev(l, u, y + dy, z, head(j)), half=half)

    def by_z(t, dy, dz, half=None):
        for j in range(2):
            deliver(t + j, 2 * dy + j, cols(dz), number(y + dy, z, head(j)), dev(l, u, y, z + dz, c), half=half)

    def got_share(slot):
        for g in range(G):
            share(slot, g).wait_recv()

    got_share(0)
    home_rows(0, 0)
    for g in range(G):
        send(0, 0, 6, g, yp).wait_recv()
        if g < 2:
            copy(panels.at[6, g], panels.at[4, g], ring_ss.at[4, g], ring_rs.at[4, g], yp).start()
        share(3, g).start()
        send(2, 0, 10, g, zp).wait_recv()
        if g < 2:
            copy(panels.at[10, g], panels.at[9, g], ring_ss.at[5, g], ring_rs.at[5, g], zp).start()
        send(1, 0, 2, g, ym).wait_recv()
        if g >= 2:
            copy(panels.at[2, g], panels.at[4, g], ring_ss.at[4, g], ring_rs.at[4, g], ym).start()
        share(1, g).start()
        send(3, 0, 8, g, zm).wait_recv()
        if g >= 2:
            copy(panels.at[8, g], panels.at[9, g], ring_ss.at[5, g], ring_rs.at[5, g], zm).start()
    got_share(1)
    got_share(3)
    home_rows(2, 1)
    home_rows(4, 3)
    home_cols(6, 1)
    home_cols(8, 3)
    by_y(10, 3, 1)
    by_y(12, 1, 3)
    by_z(14, 1, 1)
    by_z(16, 3, 3)
    for g in range(G):
        copy(panels.at[6, g], panels.at[4, g], ring_ss.at[4, g], ring_rs.at[4, g], yp).wait_recv()
        share(2, g).start()
    for g in range(G):
        copy(panels.at[10, g], panels.at[9, g], ring_ss.at[5, g], ring_rs.at[5, g], zp).wait_recv()
    home_rows(18, 2)
    by_y(20, 1, 2)
    by_y(22, 3, 2)
    got_share(2)
    home_cols(24, 2)
    by_z(26, 2, 1)
    by_z(28, 2, 3)
    by_y(30, 2, 2, 0)
    by_z(32, 2, 2, 1)

    for region in range(G):
        mine = jnp.logical_and(own, jnp.logical_and(l == region // 2, u == region % 2))

        @pl.when(jnp.logical_not(mine))
        def _():
            copy(snd.at[region], panels.at[0, r], relay_ss.at[region], relay_rs.at[r], sibling).wait_send()

    for kind in range(4):
        for g in range(G):
            send(kind, 0, 2, g, yp).wait_send()
    for kind in (4, 5):
        for g in range(G):
            send(kind, 0, 2, g, yp).wait_send()
    for slot in range(4):
        for g in range(G):
            share(slot, g).wait_send()
    for remote, maybe_self in sent:
        if maybe_self:

            @pl.when(jnp.logical_not(own))
            def _():
                remote.wait_send()
        else:
            remote.wait_send()
    for ey in range(4):
        for ez in range(4):
            for h in range(2):
                b = number(y + ey, z + ez, h)
                if (ey, ez) == (2, 2):
                    for half, sem in ((0, res_rs.at[b]), (1, res_rs.at[32 + h])):
                        part = pl.ds(half * 128, 128)
                        copy(res.at[0, part], out.at[b, part], res_ss.at[0], sem, sibling).wait_recv()
                else:
                    copy(res.at[0], out.at[b], res_ss.at[0], res_rs.at[b], sibling).wait_recv()


def gram(cent, tgt):
    dma = pltpu.SemaphoreType.DMA
    return pl.pallas_call(
        gram_kernel,
        out_shape=jax.ShapeDtypeStruct((32, B, B), jnp.float32),
        in_specs=[pl.BlockSpec(memory_space=pltpu.VMEM)] * 2,
        out_specs=pl.BlockSpec(memory_space=pl.ANY),
        scratch_shapes=[
            pltpu.VMEM((G, B, F), jnp.bfloat16),
            pltpu.VMEM((11, G, B, F), jnp.bfloat16),
            pltpu.VMEM((34, B, B), jnp.float32),
            dma((G,)),
            dma((G,)),
            dma((6, G)),
            dma((6, G)),
            dma((4, G)),
            dma((4, G)),
            dma((34,)),
            dma((34,)),
        ],
        compiler_params=pltpu.CompilerParams(
            collective_id=0, has_side_effects=True, vmem_limit_bytes=50 * 2**20
        ),
        cost_estimate=pl.CostEstimate(flops=13 * 10**9, bytes_accessed=10 * 2**20, transcendentals=0),
        name="gram",
    )(cent, tgt)


W = 512


def order_kernel(order, gt, out, rows):
    step = pl.program_id(0)

    def body(k, _):
        for i in range(8):
            rows[pl.ds(k * 8 + i, 1), :] = gt[pl.ds(order[step * W + k * 8 + i], 1), :]
        return 0

    lax.fori_loop(0, W // 8, body, 0)
    out[0] = rows[...].T


def ordered(order, gt):
    n = gt.shape[0]
    return pl.pallas_call(
        order_kernel,
        out_shape=jax.ShapeDtypeStruct((1, B, n), jnp.float32),
        grid_spec=pltpu.PrefetchScalarGridSpec(
            num_scalar_prefetch=1,
            grid=(n // W,),
            in_specs=[pl.BlockSpec((n, B), lambda i, o: (0, 0), pipeline_mode=pl.Buffered(1))],
            out_specs=pl.BlockSpec((1, B, W), lambda i, o: (0, 0, i)),
            scratch_shapes=[pltpu.VMEM((W, B), jnp.float32)],
        ),
        compiler_params=pltpu.CompilerParams(vmem_limit_bytes=40 * 2**20),
        cost_estimate=pl.CostEstimate(flops=0, bytes_accessed=2 * n * B * 4, transcendentals=0),
        name="ordered",
    )(order, gt)


def local(coords, transform, labels, subject_order):
    verts = coords.shape[2] * lax.axis_size("region")
    moved = jnp.stack(
        [
            transform[:, d, 0:1] * coords[:, 0, :]
            + transform[:, d, 1:2] * coords[:, 1, :]
            + transform[:, d, 2:3] * coords[:, 2, :]
            for d in range(3)
        ]
    )
    totals = lax.psum(jnp.sum(moved, axis=2), "region")
    cent = (moved - (totals / verts)[:, :, None]).astype(jnp.bfloat16)
    lab = labels[:, 0]
    n = lab.shape[0]
    before = jnp.arange(n)[:, None] < jnp.arange(n)[None, :]
    rank = jnp.sum(jnp.where((labels == lab[None, :]) & before, 1, 0), axis=0)
    tgt = jnp.broadcast_to((lab * CAP + rank)[None, :], (8, n))
    gt = gram(cent, tgt)
    return ordered(subject_order, gt.reshape(32 * B, B))


def solution(mesh):
    placed = (P("subj", None, "region"), P("subj", None, None), P("region", None), P())
    return jax.shard_map(
        local, mesh=mesh, in_specs=placed, out_specs=P("region", "subj", None), check_vma=False
    )
```

time: 528 us -> 210 us (0.40)
  waiting for transfers between devices: 371 us -> 0 us
  Pallas kernels: 0 us -> 196 us
  local copies, waits for them, and re-layouts: 76.1 us -> 4.23 us
  matrix products: 24.5 us -> 0 us
  blocking collectives: 29.4 us -> 5.73 us
  between operations: 13.5 us -> 0.07 us
  other arithmetic: 11.1 us -> 3.74 us
    all_gather x1 -> x0, waiting for transfers between devices: 371 us -> none  [local(): lax.all_gather(panel, 'subj', axis=0, tiled=True)]
    pallas_call x0 -> x2, Pallas kernels: none -> 196 us  [the longest x1 158 us: gram(): pl.pallas_call(gram_kernel, out_shape=jax.ShapeDtypeStruct((32, B, B), jn...]
    gather x1 -> x0, local copies, waits for them, and re-layouts: 34.9 us -> none  [local(): return jnp.take(gram_rows, subject_order, axis=2)]
    dot_general x1 -> x0, matrix products: 24.5 us -> none  [tile_block(): jnp.einsum('acgv,bcgv->gab', left, right, preferred_element_type=jnp.floa...]
    all_to_all x1 -> x0, blocking collectives: 23.7 us -> none  [local(): lax.all_to_all(buckets, 'region', split_axis=2, concat_axis=2, tiled=True)]
    scatter x1 -> x0, local copies, waits for them, and re-layouts: 13.6 us -> none  [local(): jnp.zeros((per_dev, 3, regions_count * CAP), jnp.bfloat16).at[:, :, target]]
    mul x5 -> x0, local copies, waits for them, and re-layouts: 11.1 us -> none  [the longest x1 9 us: local(): gram_rows = gram_rows * (1.0 / (3.0 * verts_total))]
    select_n x1 -> x0, local copies, waits for them, and re-layouts: 8.89 us -> none  [local(): return jnp.take(gram_rows, subject_order, axis=2)]
  transfers between devices with their start and end apart: 1 -> 0, of which waited for: 1 -> 0; matrix products, arithmetic and copies ran while one was open for 0% -> 0% of each run, Pallas kernels for 0% -> 0%
where the time goes in v1:
time: 210 us; the launch traced here: 209 us
  Pallas kernels  196 us (93%)
  blocking collectives  5.73 us (3%)
  local copies, waits for them, and re-layouts  4.23 us (2%)
  other arithmetic  3.74 us (2%)
    pallas_call x1, Pallas kernels, gram(): pl.pallas_call(gram_kernel, out_shape=jax.ShapeDtypeStruct((32, B, B), jn...  158 us
    pallas_call x1, Pallas kernels, ordered(): pl.pallas_call(order_kernel, out_shape=jax.ShapeDtypeStruct((1, B, n), jn...  37.6 us
    psum x1, blocking collectives, local(): totals = lax.psum(jnp.sum(moved, axis=2), 'region')  5.73 us

profile of v1, /device:TPU:3, one launch (start us, length us, event | category | flops | bytes accessed | tf_op | source)
XLA Modules:
  0.0 209.3 jit_solution(15059388164287788980)
XLA Ops:
  0.0 1.0 select_reduce_fusion
  1.0 0.7 multiply_add_fusion
  1.6 0.9 fusion.8
  2.5 1.7 fusion.2
  4.3 0.2 fusion
  4.4 5.7 %psum.7 = f32[3,256]{1,0:T(4,128)S(1)} all-reduce(f32[3,256]{1,0:T(4,128)S(1)} %fusion), channel_id=1, replica_groups=mesh['region'=4,'subj'=32] {'region'}, use_global_device_ids=true, to_apply=%region_1.0 | all-reduce | flops 768 | bytes 6144 | tf_op jit(solution)/shard_map/psum | solution.py:293
  10.2 0.2 subtract_convert_fusion.cent
  10.4 0.0 copy-start.1
  10.4 158.0 %gram.1 = f32[32,256,256]{2,1,0:T(8,128)} custom-call(bf16[3,256,512]{2,1,0:T(8,128)(2,1)S(1)} %subtract_convert_fusion.cent, s32[8,512]{1,0:T(8,128)S(1)} %broadcast_in_dim.19.tgt), custom_call_target="tpu_custom_call" | custom-call | flops 12999999488 | bytes 10485760 | tf_op jit(solution)/shard_map/gram/pallas_call | solution.py:224
  168.3 0.0 copy-done.1
  168.3 0.0 copy-start
  168.4 3.4 %copy-done = f32[32,256,256]{2,1,0:T(8,128)S(1)} copy-done((f32[32,256,256]{2,1,0:T(8,128)S(1)}, f32[32,256,256]{2,1,0:T(8,128)}, u32[]{:S(2)}) %copy-start) | copy-done | bytes 8388632
  171.7 37.6 %ordered.1 = f32[1,256,8192]{2,1,0:T(8,128)} custom-call(s32[8192]{0:T(1024)S(1)} %copy-done.1, f32[8192,256]{1,0:T(8,128)S(1)} %bitcast.47), custom_call_target="tpu_custom_call" | custom-call | bytes 16777216 | tf_op jit(solution)/shard_map/ordered/pallas_call | solution.py:267
  (2 shorter events, 0.0 us)
Async XLA Ops:
  10.4 158.0 %copy-start.1 = (s32[8192]{0:T(1024)S(1)}, s32[8192]{0:T(1024)}, u32[]{:S(2)}) copy-start(s32[8192]{0:T(1024)} %order.1) | copy-start | bytes 98308
  168.3 3.4 %copy-start = (f32[32,256,256]{2,1,0:T(8,128)S(1)}, f32[32,256,256]{2,1,0:T(8,128)}, u32[]{:S(2)}) copy-start(f32[32,256,256]{2,1,0:T(8,128)} %gram.1) | copy-start | bytes 25165828

commit v2 on v1

--- a/solution.py
+++ b/solution.py
@@ -19,7 +19,7 @@
     return (2 * l + c, 8 * lax.rem(y, 4) + 2 * lax.rem(z, 4) + u)
 
 
-def gram_kernel(cent, tgt, out, snd, panels, res, relay_ss, relay_rs, ring_ss, ring_rs, sib_ss, sib_rs, res_ss, res_rs):
+def gram_kernel(cent, tgt, out, out_scale, snd, panels, scales, res, relay_ss, relay_rs, ring_ss, ring_rs, sib_ss, sib_rs, res_ss, res_rs, scale_ss, scale_rs):
     r, s = lax.axis_index("region"), lax.axis_index("subj")
     l, c = r // 2, lax.rem(r, 2)
     y, z, u = s // 8, lax.rem(s // 2, 4), lax.rem(s, 2)
@@ -64,19 +64,34 @@
     yp, ym = dev(l, c, y + 1, z, u), dev(l, c, y + 3, z, u)
     zp, zm = dev(l, c, y, z + 1, u), dev(l, c, y, z + 3, u)
 
+    def piece(slot, g):
+        return scales.at[slot] if isinstance(g, int) and g == G else panels.at[slot, g]
+
     def send(kind, src, dst, g, to):
-        return copy(panels.at[src, g], panels.at[dst, g], ring_ss.at[kind, g], ring_rs.at[kind, g], to)
+        return copy(piece(src, g), piece(dst, g), ring_ss.at[kind, g], ring_rs.at[kind, g], to)
 
     def share(slot, g):
-        return copy(panels.at[2 * slot, g], panels.at[2 * slot + 1, g], sib_ss.at[slot, g], sib_rs.at[slot, g], sibling)
-
-    for g in range(G):
-        copy(snd.at[0], panels.at[0, g], relay_ss.at[0], relay_rs.at[g], sibling).wait_recv()
+        return copy(piece(2 * slot, g), piece(2 * slot + 1, g), sib_ss.at[slot, g], sib_rs.at[slot, g], sibling)
+
+    def send_own(g):
         send(0, 0, 6, g, yp).start()
         send(1, 0, 2, g, ym).start()
         send(2, 0, 10, g, zp).start()
         send(3, 0, 8, g, zm).start()
         share(0, g).start()
+
+    first = 2 * jnp.where(own, l, 1 - l)
+    turn = [lax.rem(first + i, G) for i in range(G)]
+    for g in turn:
+        copy(snd.at[0], panels.at[0, g], relay_ss.at[0], relay_rs.at[g], sibling).wait_recv()
+        send_own(g)
+    square = jnp.zeros((B, 1), jnp.float32)
+    for g in range(G):
+        x = panels[0, g].astype(jnp.float32)
+        square += jnp.sum(x * x, axis=1, keepdims=True)
+    norm = jnp.broadcast_to(jnp.sqrt(square) * (1.0 + 2.0**-7), (B, 128)).T
+    scales[0] = norm[0:16, :].astype(jnp.bfloat16)
+    send_own(G)
 
     def block(bi, ai, rows=B, at=0):
         total = None
@@ -85,7 +100,15 @@
                 panels[bi, g, at : at + rows, :], panels[ai, g], NT, preferred_element_type=jnp.float32
             )
             total = part if total is None else total + part
-        return total * (1.0 / (3.0 * 2048))
+        inv_a, inv_b = inverse(ai), inverse(bi)
+        column = jnp.broadcast_to(inv_b, (128, B)).T[at : at + rows]
+        wide = jnp.concatenate([column, column], axis=1)
+        scaled = total * wide * (inv_a * 32767.0)
+        return (scaled + 12582912.0 - 12582912.0).astype(jnp.int32).astype(jnp.int16)
+
+    def inverse(slot):
+        row = scales[slot].astype(jnp.float32)[0:1, :]
+        return jnp.where(row > 0.0, 1.0 / row, 0.0)
 
     def number(yb, zb, hb):
         return 8 * lax.rem(yb, 4) + 2 * lax.rem(zb, 4) + hb
@@ -101,19 +124,23 @@
             res[t, part, :] = block(bi, ai, 128, half * 128)
             src, dst = res.at[t, part], out.at[b, part]
             sem = res_rs.at[b] if half == 0 else res_rs.at[32 + lax.rem(b, 2)]
-        remote = copy(src, dst, res_ss.at[t], sem, owner)
-        if maybe_self:
-
-            @pl.when(own)
-            def _():
-                pltpu.make_async_copy(src, dst, sem).start()
-
-            @pl.when(jnp.logical_not(own))
-            def _():
+        moves = [(src, dst, res_ss.at[t], sem)]
+        if half != 1:
+            moves.append((scales.at[bi], out_scale.at[b], scale_ss.at[t], scale_rs.at[b]))
+        for src, dst, ss, rs in moves:
+            remote = copy(src, dst, ss, rs, owner)
+            if maybe_self:
+
+                @pl.when(own)
+                def _():
+                    pltpu.make_async_copy(src, dst, rs).start()
+
+                @pl.when(jnp.logical_not(own))
+                def _():
+                    remote.start()
+            else:
                 remote.start()
-        else:
-            remote.start()
-        sent.append((remote, maybe_self))
+            sent.append((remote, maybe_self))
 
     def cols(dz):
         return 0 if dz == 0 else 7 + dz
@@ -138,26 +165,30 @@
             deliver(t + j, 2 * dy + j, cols(dz), number(y + dy, z, head(j)), dev(l, u, y, z + dz, c), half=half)
 
     def got_share(slot):
-        for g in range(G):
+        for g in range(G + 1):
             share(slot, g).wait_recv()
+
+    def forward(kind, src, dst, g, to):
+        return copy(piece(src, g), piece(dst, g), ring_ss.at[kind, g], ring_rs.at[kind, g], to)
 
     got_share(0)
     home_rows(0, 0)
-    for g in range(G):
+    for i, g in enumerate(turn + [G]):
+        up = i % 2 == 0
         send(0, 0, 6, g, yp).wait_recv()
-        if g < 2:
-            copy(panels.at[6, g], panels.at[4, g], ring_ss.at[4, g], ring_rs.at[4, g], yp).start()
+        if up:
+            forward(4, 6, 4, g, yp).start()
         share(3, g).start()
         send(2, 0, 10, g, zp).wait_recv()
-        if g < 2:
-            copy(panels.at[10, g], panels.at[9, g], ring_ss.at[5, g], ring_rs.at[5, g], zp).start()
+        if up:
+            forward(5, 10, 9, g, zp).start()
         send(1, 0, 2, g, ym).wait_recv()
-        if g >= 2:
-            copy(panels.at[2, g], panels.at[4, g], ring_ss.at[4, g], ring_rs.at[4, g], ym).start()
+        if not up:
+            forward(4, 2, 4, g, ym).start()
         share(1, g).start()
         send(3, 0, 8, g, zm).wait_recv()
-        if g >= 2:
-            copy(panels.at[8, g], panels.at[9, g], ring_ss.at[5, g], ring_rs.at[5, g], zm).start()
+        if not up:
+            forward(5, 8, 9, g, zm).start()
     got_share(1)
     got_share(3)
     home_rows(2, 1)
@@ -168,11 +199,11 @@
     by_y(12, 1, 3)
     by_z(14, 1, 1)
     by_z(16, 3, 3)
-    for g in range(G):
-        copy(panels.at[6, g], panels.at[4, g], ring_ss.at[4, g], ring_rs.at[4, g], yp).wait_recv()
+    for g in turn + [G]:
+        forward(4, 6, 4, g, yp).wait_recv()
         share(2, g).start()
-    for g in range(G):
-        copy(panels.at[10, g], panels.at[9, g], ring_ss.at[5, g], ring_rs.at[5, g], zp).wait_recv()
+    for g in turn + [G]:
+        forward(5, 10, 9, g, zp).wait_recv()
     home_rows(18, 2)
     by_y(20, 1, 2)
     by_y(22, 3, 2)
@@ -190,14 +221,10 @@
         def _():
             copy(snd.at[region], panels.at[0, r], relay_ss.at[region], relay_rs.at[r], sibling).wait_send()
 
-    for kind in range(4):
-        for g in range(G):
+    for g in range(G + 1):
+        for kind in range(6):
             send(kind, 0, 2, g, yp).wait_send()
-    for kind in (4, 5):
-        for g in range(G):
-            send(kind, 0, 2, g, yp).wait_send()
-    for slot in range(4):
-        for g in range(G):
+        for slot in range(4):
             share(slot, g).wait_send()
     for remote, maybe_self in sent:
         if maybe_self:
@@ -211,6 +238,7 @@
         for ez in range(4):
             for h in range(2):
                 b = number(y + ey, z + ez, h)
+                copy(scales.at[0], out_scale.at[b], scale_ss.at[0], scale_rs.at[b], sibling).wait_recv()
                 if (ey, ez) == (2, 2):
                     for half, sem in ((0, res_rs.at[b]), (1, res_rs.at[32 + h])):
                         part = pl.ds(half * 128, 128)
@@ -223,21 +251,27 @@
     dma = pltpu.SemaphoreType.DMA
     return pl.pallas_call(
         gram_kernel,
-        out_shape=jax.ShapeDtypeStruct((32, B, B), jnp.float32),
+        out_shape=(
+            jax.ShapeDtypeStruct((32, B, B), jnp.int16),
+            jax.ShapeDtypeStruct((32, 16, B), jnp.bfloat16),
+        ),
         in_specs=[pl.BlockSpec(memory_space=pltpu.VMEM)] * 2,
-        out_specs=pl.BlockSpec(memory_space=pl.ANY),
+        out_specs=[pl.BlockSpec(memory_space=pl.ANY)] * 2,
         scratch_shapes=[
             pltpu.VMEM((G, B, F), jnp.bfloat16),
             pltpu.VMEM((11, G, B, F), jnp.bfloat16),
-            pltpu.VMEM((34, B, B), jnp.float32),
+            pltpu.VMEM((11, 16, B), jnp.bfloat16),
+            pltpu.VMEM((34, B, B), jnp.int16),
             dma((G,)),
             dma((G,)),
-            dma((6, G)),
-            dma((6, G)),
-            dma((4, G)),
-            dma((4, G)),
+            dma((6, G + 1)),
+            dma((6, G + 1)),
+            dma((4, G + 1)),
+            dma((4, G + 1)),
             dma((34,)),
             dma((34,)),
+            dma((34,)),
+            dma((32,)),
         ],
         compiler_params=pltpu.CompilerParams(
             collective_id=0, has_side_effects=True, vmem_limit_bytes=50 * 2**20
@@ -247,37 +281,70 @@
     )(cent, tgt)
 
 
-W = 512
-
-
-def order_kernel(order, gt, out, rows):
+W = 1024
+T = 128
+U = 16
+
+
+def order_kernel(order, me, q, scale, out, table, even, odd):
     step = pl.program_id(0)
 
-    def body(k, _):
-        for i in range(8):
-            rows[pl.ds(k * 8 + i, 1), :] = gt[pl.ds(order[step * W + k * 8 + i], 1), :]
-        return 0
-
-    lax.fori_loop(0, W // 8, body, 0)
-    out[0] = rows[...].T
-
-
-def ordered(order, gt):
-    n = gt.shape[0]
+    @pl.when(step == 0)
+    def _():
+        row = scale[me[0]].astype(jnp.float32)[0:1, :] * (1.0 / (32767.0 * 3.0 * 2048.0))
+
+        def decode(b, _):
+            column = jnp.broadcast_to(scale[b].astype(jnp.float32)[0:1, :], (128, B)).T
+            for i in range(2):
+                lanes = slice(128 * i, 128 * (i + 1))
+                values = q[b, :, lanes].astype(jnp.int32).astype(jnp.float32)
+                table[pl.ds(b * 2 * B + i, B, stride=2), :] = values * column * row[:, lanes]
+            return 0
+
+        lax.fori_loop(0, q.shape[0], decode, 0)
+
+    def gather(rows, t):
+        for k in range(0, T, U):
+            at = step * W + t * T + k
+            loaded = [table[pl.ds(pl.multiple_of(2 * order[at + i], 2), 2), :] for i in range(U)]
+            for i in range(U):
+                rows[pl.ds(2 * (k + i), 2), :] = loaded[i]
+
+    def flip(rows, t):
+        for i in range(2):
+            out[0, 128 * i : 128 * (i + 1), t * T : (t + 1) * T] = rows[pl.ds(i, T, stride=2), :].T
+
+    both = (even, odd)
+    gather(even, 0)
+    for t in range(1, W // T):
+        flip(both[(t - 1) % 2], t - 1)
+        gather(both[t % 2], t)
+    flip(both[(W // T - 1) % 2], W // T - 1)
+
+
+def ordered(order, me, q, scale):
+    n = order.shape[0]
     return pl.pallas_call(
         order_kernel,
         out_shape=jax.ShapeDtypeStruct((1, B, n), jnp.float32),
         grid_spec=pltpu.PrefetchScalarGridSpec(
-            num_scalar_prefetch=1,
+            num_scalar_prefetch=2,
             grid=(n // W,),
-            in_specs=[pl.BlockSpec((n, B), lambda i, o: (0, 0), pipeline_mode=pl.Buffered(1))],
-            out_specs=pl.BlockSpec((1, B, W), lambda i, o: (0, 0, i)),
-            scratch_shapes=[pltpu.VMEM((W, B), jnp.float32)],
+            in_specs=[
+                pl.BlockSpec(q.shape, lambda i, o, m: (0, 0, 0), pipeline_mode=pl.Buffered(1)),
+                pl.BlockSpec(scale.shape, lambda i, o, m: (0, 0, 0), pipeline_mode=pl.Buffered(1)),
+            ],
+            out_specs=pl.BlockSpec((1, B, W), lambda i, o, m: (0, 0, i)),
+            scratch_shapes=[
+                pltpu.VMEM((2 * n, 128), jnp.float32),
+                pltpu.VMEM((2 * T, 128), jnp.float32),
+                pltpu.VMEM((2 * T, 128), jnp.float32),
+            ],
         ),
         compiler_params=pltpu.CompilerParams(vmem_limit_bytes=40 * 2**20),
-        cost_estimate=pl.CostEstimate(flops=0, bytes_accessed=2 * n * B * 4, transcendentals=0),
+        cost_estimate=pl.CostEstimate(flops=0, bytes_accessed=6 * n * B, transcendentals=0),
         name="ordered",
-    )(order, gt)
+    )(order, me, q, scale)
 
 
 def local(coords, transform, labels, subject_order):
@@ -297,8 +364,7 @@
     before = jnp.arange(n)[:, None] < jnp.arange(n)[None, :]
     rank = jnp.sum(jnp.where((labels == lab[None, :]) & before, 1, 0), axis=0)
     tgt = jnp.broadcast_to((lab * CAP + rank)[None, :], (8, n))
-    gt = gram(cent, tgt)
-    return ordered(subject_order, gt.reshape(32 * B, B))
+    return ordered(subject_order, lax.axis_index("subj")[None], *gram(cent, tgt))
 
 
 def solution(mesh):

time: 210 us -> 144 us (0.69)
  Pallas kernels: 196 us -> 131 us
    pallas_call x1, Pallas kernels: 158 us -> 116 us  [gram(): pl.pallas_call(gram_kernel, out_shape=(jax.ShapeDtypeStruct((32, B, B), j...]
    pallas_call x1, Pallas kernels: 37.6 us -> 15.5 us  [ordered(): pl.pallas_call(order_kernel, out_shape=jax.ShapeDtypeStruct((1, B, n), jn...]
where the time goes in v2:
time: 144 us
  Pallas kernels  131 us (91%)
  blocking collectives  5.73 us (4%)
  other arithmetic  3.74 us (3%)
  local copies, waits for them, and re-layouts  3.04 us (2%)
    pallas_call x1, Pallas kernels, gram(): pl.pallas_call(gram_kernel, out_shape=(jax.ShapeDtypeStruct((32, B, B), j...  116 us
    pallas_call x1, Pallas kernels, ordered(): pl.pallas_call(order_kernel, out_shape=jax.ShapeDtypeStruct((1, B, n), jn...  15.5 us
    psum x1, blocking collectives, local(): totals = lax.psum(jnp.sum(moved, axis=2), 'region')  5.73 us

profile of v2, /device:TPU:3, one launch (start us, length us, event | category | flops | bytes accessed | tf_op | source)
XLA Modules:
  0.0 144.0 jit_solution(1256371897821463809)
XLA Ops:
  0.0 1.0 select_reduce_fusion
  1.0 0.7 multiply_add_fusion
  1.6 0.9 fusion.8
  2.5 1.7 %fusion.2 = (f32[1,256,512]{2,1,0:T(8,128)S(1)}, f32[1,256,512]{2,1,0:T(8,128)S(1)}, f32[1,256,512]{2,1,0:T(8,128)S(1)}) fusion(f32[256,3,512]{2,0,1:T(8,128)} %param.4, f32[256]{0:T(256)S(1)} %bitcast.54, f32[256]{0:T(256)S(1)} %bitcast.55, f32[256]{0:T(256)S(1)} %bitcast.49, f32[256]{0:T(256)S(1)} %bitcast.51, f32[256]{0:T(256)S(1)} %bitcast.52, ...), kind=kLoop, calls=%fused_computation.9 | loop fusion | flops 1966080 | bytes 3154944 | tf_op jit(solution)/shard_map/add | solution.py:354
  4.3 0.2 fusion
  4.4 5.7 %psum.7 = f32[3,256]{1,0:T(4,128)S(1)} all-reduce(f32[3,256]{1,0:T(4,128)S(1)} %fusion), channel_id=1, replica_groups=mesh['region'=4,'subj'=32] {'region'}, use_global_device_ids=true, to_apply=%region_1.0 | all-reduce | flops 768 | bytes 6144 | tf_op jit(solution)/shard_map/psum | solution.py:360
  10.2 0.2 subtract_convert_fusion.cent
  10.4 0.0 copy-start.1
  10.4 115.9 %gram.1 = (s16[32,256,256]{2,1,0:T(8,128)(2,1)}, bf16[32,16,256]{2,1,0:T(8,128)(2,1)S(1)}) custom-call(bf16[3,256,512]{2,1,0:T(8,128)(2,1)S(1)} %subtract_convert_fusion.cent, s32[8,512]{1,0:T(8,128)S(1)} %broadcast_in_dim.23.tgt), custom_call_target="tpu_custom_call" | custom-call | flops 12999999488 | bytes 10485760 | tf_op jit(solution)/shard_map/gram/pallas_call | solution.py:252
  126.3 0.0 copy-done.1
  126.3 0.0 copy-start
  126.3 2.2 %copy-done = s16[32,256,256]{2,1,0:T(8,128)(2,1)S(1)} copy-done((s16[32,256,256]{2,1,0:T(8,128)(2,1)S(1)}, s16[32,256,256]{2,1,0:T(8,128)(2,1)}, u32[]{:S(2)}) %copy-start) | copy-done | bytes 4194328
  128.5 15.5 %ordered.1 = f32[1,256,8192]{2,1,0:T(8,128)} custom-call(s32[8192]{0:T(1024)S(1)} %copy-done.1, s32[1]{0:T(128)} %bitcast.me, s16[32,256,256]{2,1,0:T(8,128)(2,1)S(1)} %copy-done, bf16[32,16,256]{2,1,0:T(8,128)(2,1)S(1)} %get-tuple-element.8.scale), custom_call_target="tpu_custom_call" | custom-call | bytes 12582912 | tf_op jit(solution)/shard_map/ordered/pallas_call | solution.py:327
  (2 shorter events, 0.0 us)
Async XLA Ops:
  10.4 116.0 %copy-start.1 = (s32[8192]{0:T(1024)S(1)}, s32[8192]{0:T(1024)}, u32[]{:S(2)}) copy-start(s32[8192]{0:T(1024)} %order.1) | copy-start | bytes 98308
  126.3 2.2 %copy-start = (s16[32,256,256]{2,1,0:T(8,128)(2,1)S(1)}, s16[32,256,256]{2,1,0:T(8,128)(2,1)}, u32[]{:S(2)}) copy-start(s16[32,256,256]{2,1,0:T(8,128)(2,1)} %get-tuple-element.7.q) | copy-start | bytes 12582916

commit v3 on v0

v3 whole, which is shorter than its diff:
```python
import functools

import jax
import jax.numpy as jnp
from jax import lax
from jax.experimental import pallas as pl
from jax.experimental.pallas import tpu as pltpu
from jax.sharding import PartitionSpec as P

CAP = 256
B = 256
H = 128
G = 4
F = 3 * CAP
MESH = pl.DeviceIdType.MESH
NT = (((1,), (1,)), ((), ()))


def dev(l, c, y, z, u):
    return (2 * l + c, 8 * lax.rem(y, 4) + 2 * lax.rem(z, 4) + u)


def gram_kernel(cent, tgt, out, out_scale, snd, panels, scales, res, relay_ss, relay_rs, ring_ss, ring_rs, sib_ss, sib_rs, res_ss, res_rs, scale_ss, scale_rs):
    r, s = lax.axis_index("region"), lax.axis_index("subj")
    l, c = r // 2, lax.rem(r, 2)
    y, z, u = s // 8, lax.rem(s // 2, 4), lax.rem(s, 2)
    barrier = pltpu.get_barrier_semaphore()
    own = c == u

    def copy(src, dst, ss, rs, to):
        return pltpu.make_async_remote_copy(
            src_ref=src, dst_ref=dst, send_sem=ss, recv_sem=rs, device_id=to, device_id_type=MESH
        )

    for k in range(1, 8):
        q = lax.rem(l * 4 + c * 2 + u + k, 8)
        pl.semaphore_signal(barrier, inc=1, device_id=dev(q // 4, lax.rem(q // 2, 2), y, z, lax.rem(q, 2)), device_id_type=MESH)
    for k in range(1, 4):
        for cc in range(2):
            for uu in range(2):
                pl.semaphore_signal(barrier, inc=1, device_id=dev(l, cc, y + k, z, uu), device_id_type=MESH)
                pl.semaphore_signal(barrier, inc=1, device_id=dev(l, cc, y, z + k, uu), device_id_type=MESH)
    pl.semaphore_wait(barrier, 31)

    def relay(half, region):
        lr, ur = region // 2, region % 2
        mine = jnp.logical_and(own, jnp.logical_and(l == lr, u == ur))
        src, dst, rs = snd.at[half, region], panels.at[r, 0, half], relay_rs.at[half, r]
        return mine, src, dst, rs, copy(src, dst, relay_ss.at[half, region], rs, dev(lr, u, y, z, ur))

    row = tgt[0:1, :]
    slots = lax.broadcasted_iota(jnp.int32, (CAP, row.shape[1]), 0)
    for half in range(2):
        for region in range(G):
            pick = jnp.where(slots + region * CAP == row, 1.0, 0.0).astype(jnp.bfloat16)
            for d in range(3):
                snd[half, region, :, d * CAP : (d + 1) * CAP] = lax.dot_general(
                    cent[d, half * H : (half + 1) * H, :], pick, NT, preferred_element_type=jnp.float32
                ).astype(jnp.bfloat16)
            mine, src, dst, rs, remote = relay(half, region)

            @pl.when(mine)
            def _():
                pltpu.make_async_copy(src, dst, rs).start()

            @pl.when(jnp.logical_not(mine))
            def _():
                remote.start()

    sibling = dev(l, 1 - c, y, z, u)
    yp, ym = dev(l, c, y + 1, z, u), dev(l, c, y + 3, z, u)
    zp, zm = dev(l, c, y, z + 1, u), dev(l, c, y, z + 3, u)

    def piece(slot, half, g):
        return scales.at[half, slot] if isinstance(g, int) and g == G else panels.at[g, slot, half]

    def place(slot):
        dy, dz = {2: 1, 4: 3, 6: 2}.get(slot // 2 * 2, 0), {8: 1, 9: 3, 10: 2}.get(slot, 0)
        return (y + (dy if slot < 8 else 0), z + dz, c if slot >= 8 or slot % 2 == 0 else 1 - c)

    def send(kind, src, dst, half, g, to):
        at = (kind, half, g)
        return copy(piece(src, half, g), piece(dst, half, g), ring_ss.at[at], ring_rs.at[at], to)

    def share(pos, half, g):
        at = (pos, half, g)
        return copy(piece(2 * pos, half, g), piece(2 * pos + 1, half, g), sib_ss.at[at], sib_rs.at[at], sibling)

    def send_own(half, g):
        send(0, 0, 4, half, g, yp).start()
        send(1, 0, 2, half, g, ym).start()
        send(2, 0, 9, half, g, zp).start()
        send(3, 0, 8, half, g, zm).start()
        share(0, half, g).start()

    first = 2 * jnp.where(own, l, 1 - l)
    turn = [lax.rem(first + i, G) for i in range(G)]
    for half in range(2):
        for g in turn:
            copy(snd.at[0, 0], panels.at[g, 0, half], relay_ss.at[0, 0], relay_rs.at[half, g], sibling).wait_recv()
            send_own(half, g)
        square = jnp.zeros((H, 1), jnp.float32)
        for g in range(G):
            x = panels[g, 0, half].astype(jnp.float32)
            square += jnp.sum(x * x, axis=1, keepdims=True)
        norm = jnp.broadcast_to(jnp.sqrt(square) * (1.0 + 2.0**-7), (H, 128)).T
        scales[half, 0] = norm[0:16, :].astype(jnp.bfloat16)
        send_own(half, G)

    def inverse(half, slot):
        row = scales[half, slot].astype(jnp.float32)[0:1, :]
        return jnp.where(row > 0.0, 1.0 / row, 0.0)

    def products(bs, b_halves, as_, a_halves):
        def rows(g, slots, halves):
            some = slice(halves[0], halves[-1] + 1)
            return panels[g, slots, some].reshape(-1, F)

        def inverses(slots, halves):
            return [inverse(half, k) for k in range(slots.start, slots.stop) for half in halves]

        total = None
        for g in range(G):
            part = lax.dot_general(rows(g, bs, b_halves), rows(g, as_, a_halves), NT, preferred_element_type=jnp.float32)
            total = part if total is None else total + part
        across, down = inverses(as_, a_halves), inverses(bs, b_halves)
        down = [jnp.broadcast_to(v, (128, H)).T for v in down]
        return [
            [
                total[i * H : (i + 1) * H, k * H : (k + 1) * H] * down[i] * (across[k] * 32767.0) + 12582912.0 - 12582912.0
                for k in range(len(across))
            ]
            for i in range(len(down))
        ]

    blocks = {}

    def deliver(b, hb, a, a_halves, tiles):
        number = 8 * lax.rem(place(b)[0], 4) + 2 * lax.rem(place(b)[1], 4) + place(b)[2]
        owner = dev(l, u, *place(a))
        t, b_halves = blocks.setdefault((b, a), (len(blocks), set()))
        b_halves.add(hb)
        at = (pl.ds(hb * H, H), pl.ds(a_halves[0] * H, len(a_halves) * H))
        for ha, tile in zip(a_halves, tiles, strict=True):
            res[t, hb * H : (hb + 1) * H, ha * H : (ha + 1) * H] = tile.astype(jnp.int32).astype(jnp.int16)
        moves = [(res.at[(t, *at)], out.at[(number, *at)], res_ss.at[t], res_rs.at[number])]
        if 0 in a_halves:
            moves.append((scales.at[hb, b], out_scale.at[number, hb], scale_ss.at[t], scale_rs.at[number]))
        for src, dst, ss, rs in moves:
            remote = copy(src, dst, ss, rs, owner)
            if a == 0:

                @pl.when(own)
                def _():
                    pltpu.make_async_copy(src, dst, rs).start()

                @pl.when(jnp.logical_not(own))
                def _():
                    remote.start()
            else:
                remote.start()

    BOTH = (0, 1)

    def straight(bs, b_halves, as_, a_halves, keep=lambda b, a: True):
        out_of = products(bs, b_halves, as_, a_halves)
        n, m = len(b_halves), len(a_halves)
        for i, b in enumerate(range(bs.start, bs.stop)):
            for p, hb in enumerate(b_halves):
                for k, a in enumerate(range(as_.start, as_.stop)):
                    if keep(b, a):
                        deliver(b, hb, a, a_halves, out_of[i * n + p][k * m : (k + 1) * m])
        return out_of

    def turned(out_of, bs, b_halves, as_, a_halves, keep=lambda b, a: True):
        n, m = len(b_halves), len(a_halves)
        for k, a in enumerate(range(as_.start, as_.stop)):
            for q, ha in enumerate(a_halves):
                for i, b in enumerate(range(bs.start, bs.stop)):
                    if keep(b, a):
                        deliver(a, ha, b, b_halves, [out_of[i * n + p][k * m + q].T for p in range(n)])

    def got_share(pos, half):
        for g in range(G + 1):
            share(pos, half, g).wait_recv()

    for half in range(2):
        got_share(0, half)
    straight(slice(0, 1), BOTH, slice(0, 2), BOTH)
    for half in range(2):
        for i, g in enumerate(turn + [G]):
            up = i % 2 == 0
            send(0, 0, 4, half, g, yp).wait_recv()
            if up:
                send(4, 4, 6, half, g, yp).start()
            share(2, half, g).start()
            send(2, 0, 9, half, g, zp).wait_recv()
            if up:
                send(5, 9, 10, half, g, zp).start()
            send(1, 0, 2, half, g, ym).wait_recv()
            if not up:
                send(4, 2, 6, half, g, ym).start()
            share(1, half, g).start()
            send(3, 0, 8, half, g, zm).wait_recv()
            if not up:
                send(5, 8, 10, half, g, zm).start()
        straight(slice(8, 10), (half,), slice(0, 2), BOTH)
        got_share(1, half)
        got_share(2, half)
        straight(slice(2, 6), (half,), slice(0, 1), BOTH)
        for hb, has in (((0,), (0,)),) if half == 0 else (((1,), BOTH), ((0,), (1,))):
            cross = slice(8, 10), hb, slice(4, 6), has
            turned(straight(*cross), *cross)
    for half in range(2):
        here = (half,)
        for g in turn + [G]:
            send(4, 4, 6, half, g, yp).wait_recv()
            share(3, half, g).start()
        for g in turn + [G]:
            send(5, 9, 10, half, g, zp).wait_recv()
        far = slice(0, 6), BOTH, slice(10, 11), here
        turned(products(*far), *far)
        got_share(3, half)
        straight(slice(6, 8), here, slice(0, 1), BOTH)
        straight(slice(6, 8), here, slice(8, 10), BOTH)
        if half == 0:
            straight(slice(10, 11), (0,), slice(6, 8), (0,))
        else:
            opposite = slice(6, 8), (1,), slice(10, 11), BOTH
            tiles = straight(*opposite)
            turned([row[:1] for row in tiles], slice(6, 8), (1,), slice(10, 11), (0,))

    for half in range(2):
        for region in range(G):
            mine, *_, remote = relay(half, region)

            @pl.when(jnp.logical_not(mine))
            def _():
                remote.wait_send()

        for g in range(G + 1):
            for kind in range(6):
                send(kind, 0, 2, half, g, yp).wait_send()
            for pos in range(4):
                share(pos, half, g).wait_send()
    for (_, a), (t, halves) in blocks.items():
        part = pl.ds(min(halves) * H, len(halves) * H)
        some = pl.ds(min(halves), len(halves))

        def left(t=t, part=part, some=some):
            copy(res.at[t, part], out.at[0, part], res_ss.at[t], res_rs.at[0], sibling).wait_send()
            copy(out_scale.at[0, some], out_scale.at[0, some], scale_ss.at[t], scale_rs.at[0], sibling).wait_send()

        if a == 0:
            pl.when(jnp.logical_not(own))(left)
        else:
            left()
    for b in range(32):
        copy(res.at[0], out.at[b], res_ss.at[0], res_rs.at[b], sibling).wait_recv()
        copy(out_scale.at[b], out_scale.at[b], scale_ss.at[0], scale_rs.at[b], sibling).wait_recv()


def gram(cent, tgt):
    dma = pltpu.SemaphoreType.DMA
    return pl.pallas_call(
        gram_kernel,
        out_shape=(
            jax.ShapeDtypeStruct((32, B, B), jnp.int16),
            jax.ShapeDtypeStruct((32, 2, 16, H), jnp.bfloat16),
        ),
        in_specs=[pl.BlockSpec(memory_space=pltpu.VMEM)] * 2,
        out_specs=[pl.BlockSpec(memory_space=pl.ANY)] * 2,
        scratch_shapes=[
            pltpu.VMEM((2, G, H, F), jnp.bfloat16),
            pltpu.VMEM((G, 11, 2, H, F), jnp.bfloat16),
            pltpu.VMEM((2, 11, 16, H), jnp.bfloat16),
            pltpu.VMEM((34, B, B), jnp.int16),
            dma((2, G)),
            dma((2, G)),
            dma((6, 2, G + 1)),
            dma((6, 2, G + 1)),
            dma((4, 2, G + 1)),
            dma((4, 2, G + 1)),
            dma((34,)),
            dma((32,)),
            dma((34,)),
            dma((32,)),
        ],
        compiler_params=pltpu.CompilerParams(
            collective_id=0, has_side_effects=True, vmem_limit_bytes=50 * 2**20
        ),
        cost_estimate=pl.CostEstimate(flops=13 * 10**9, bytes_accessed=10 * 2**20, transcendentals=0),
        name="gram",
    )(cent, tgt)


W = 1024
T = 128
U = 16


def order_kernel(order, me, q, scale, out, table, even, odd):
    step = pl.program_id(0)

    @pl.when(step == 0)
    def _():
        def scale_row(b):
            halves = [scale[b, half].astype(jnp.float32)[0:1, :] for half in range(2)]
            return jnp.concatenate(halves, axis=1)

        row = scale_row(me[0]) * (1.0 / (32767.0 * 3.0 * 2048.0))

        def decode(b, _):
            column = jnp.broadcast_to(scale_row(b), (128, B)).T
            for i in range(2):
                lanes = slice(128 * i, 128 * (i + 1))
                values = q[b, :, lanes].astype(jnp.int32).astype(jnp.float32)
                table[pl.ds(b * 2 * B + i, B, stride=2), :] = values * column * row[:, lanes]
            return 0

        lax.fori_loop(0, q.shape[0], decode, 0)

    def gather(rows, t):
        for k in range(0, T, U):
            at = step * W + t * T + k
            loaded = [table[pl.ds(pl.multiple_of(2 * order[at + i], 2), 2), :] for i in range(U)]
            for i in range(U):
                rows[pl.ds(2 * (k + i), 2), :] = loaded[i]

    def flip(rows, t):
        for i in range(2):
            out[0, 128 * i : 128 * (i + 1), t * T : (t + 1) * T] = rows[pl.ds(i, T, stride=2), :].T

    both = (even, odd)
    gather(even, 0)
    for t in range(1, W // T):
        flip(both[(t - 1) % 2], t - 1)
        gather(both[t % 2], t)
    flip(both[(W // T - 1) % 2], W // T - 1)


def ordered(order, me, q, scale):
    n = order.shape[0]
    return pl.pallas_call(
        order_kernel,
        out_shape=jax.ShapeDtypeStruct((1, B, n), jnp.float32),
        grid_spec=pltpu.PrefetchScalarGridSpec(
            num_scalar_prefetch=2,
            grid=(n // W,),
            in_specs=[
                pl.BlockSpec(q.shape, lambda i, o, m: (0, 0, 0), pipeline_mode=pl.Buffered(1)),
                pl.BlockSpec(scale.shape, lambda i, o, m: (0, 0, 0, 0), pipeline_mode=pl.Buffered(1)),
            ],
            out_specs=pl.BlockSpec((1, B, W), lambda i, o, m: (0, 0, i)),
            scratch_shapes=[
                pltpu.VMEM((2 * n, 128), jnp.float32),
                pltpu.VMEM((2 * T, 128), jnp.float32),
                pltpu.VMEM((2 * T, 128), jnp.float32),
            ],
        ),
        compiler_params=pltpu.CompilerParams(vmem_limit_bytes=40 * 2**20),
        cost_estimate=pl.CostEstimate(flops=0, bytes_accessed=6 * n * B, transcendentals=0),
        name="ordered",
    )(order, me, q, scale)


def local(coords, transform, labels, subject_order):
    verts = coords.shape[2] * lax.axis_size("region")
    moved = jnp.stack(
        [
            transform[:, d, 0:1] * coords[:, 0, :]
            + transform[:, d, 1:2] * coords[:, 1, :]
            + transform[:, d, 2:3] * coords[:, 2, :]
            for d in range(3)
        ]
    )
    totals = lax.psum(jnp.sum(moved, axis=2), "region")
    cent = (moved - (totals / verts)[:, :, None]).astype(jnp.bfloat16)
    lab = labels[:, 0]
    n = lab.shape[0]
    before = jnp.arange(n)[:, None] < jnp.arange(n)[None, :]
    rank = jnp.sum(jnp.where((labels == lab[None, :]) & before, 1, 0), axis=0)
    tgt = jnp.broadcast_to((lab * CAP + rank)[None, :], (8, n))
    return ordered(subject_order, lax.axis_index("subj")[None], *gram(cent, tgt))


def solution(mesh):
    placed = (P("subj", None, "region"), P("subj", None, None), P("region", None), P())
    return jax.shard_map(
        local, mesh=mesh, in_specs=placed, out_specs=P("region", "subj", None), check_vma=False
    )
```

time: 528 us -> 133 us (0.25)
  waiting for transfers between devices: 371 us -> 0 us
  Pallas kernels: 0 us -> 120 us
  local copies, waits for them, and re-layouts: 76.1 us -> 3.04 us
  matrix products: 24.5 us -> 0 us
  blocking collectives: 29.4 us -> 5.73 us
  between operations: 13.5 us -> 0.07 us
  other arithmetic: 11.1 us -> 3.74 us
    all_gather x1 -> x0, waiting for transfers between devices: 371 us -> none  [local(): lax.all_gather(panel, 'subj', axis=0, tiled=True)]
    pallas_call x0 -> x2, Pallas kernels: none -> 120 us  [the longest x1 104 us: gram(): pl.pallas_call(gram_kernel, out_shape=(jax.ShapeDtypeStruct((32, B, B), j...]
    gather x1 -> x0, local copies, waits for them, and re-layouts: 34.9 us -> none  [local(): return jnp.take(gram_rows, subject_order, axis=2)]
    dot_general x1 -> x0, matrix products: 24.5 us -> none  [tile_block(): jnp.einsum('acgv,bcgv->gab', left, right, preferred_element_type=jnp.floa...]
    all_to_all x1 -> x0, blocking collectives: 23.7 us -> none  [local(): lax.all_to_all(buckets, 'region', split_axis=2, concat_axis=2, tiled=True)]
    scatter x1 -> x0, local copies, waits for them, and re-layouts: 13.6 us -> none  [local(): jnp.zeros((per_dev, 3, regions_count * CAP), jnp.bfloat16).at[:, :, target]]
    mul x5 -> x0, local copies, waits for them, and re-layouts: 11.1 us -> none  [the longest x1 9 us: local(): gram_rows = gram_rows * (1.0 / (3.0 * verts_total))]
    select_n x1 -> x0, local copies, waits for them, and re-layouts: 8.89 us -> none  [local(): return jnp.take(gram_rows, subject_order, axis=2)]
  transfers between devices with their start and end apart: 1 -> 0, of which waited for: 1 -> 0; matrix products, arithmetic and copies ran while one was open for 0% -> 0% of each run, Pallas kernels for 0% -> 0%
where the time goes in v3:
time: 133 us; the launch traced here: 132 us
  Pallas kernels  120 us (90%)
  blocking collectives  5.73 us (4%)
  other arithmetic  3.74 us (3%)
  local copies, waits for them, and re-layouts  3.04 us (2%)
    pallas_call x1, Pallas kernels, gram(): pl.pallas_call(gram_kernel, out_shape=(jax.ShapeDtypeStruct((32, B, B), j...  104 us
    pallas_call x1, Pallas kernels, ordered(): pl.pallas_call(order_kernel, out_shape=jax.ShapeDtypeStruct((1, B, n), jn...  15.5 us
    psum x1, blocking collectives, local(): totals = lax.psum(jnp.sum(moved, axis=2), 'region')  5.73 us

profile of v3, /device:TPU:3, one launch (start us, length us, event | category | flops | bytes accessed | tf_op | source)
XLA Modules:
  0.0 132.3 jit_solution(3054400278600501106)
XLA Ops:
  0.0 1.0 select_reduce_fusion
  1.0 0.7 multiply_add_fusion
  1.6 0.9 fusion.8
  2.5 1.7 %fusion.2 = (f32[1,256,512]{2,1,0:T(8,128)S(1)}, f32[1,256,512]{2,1,0:T(8,128)S(1)}, f32[1,256,512]{2,1,0:T(8,128)S(1)}) fusion(f32[256,3,512]{2,0,1:T(8,128)} %param.4, f32[256]{0:T(256)S(1)} %bitcast.54, f32[256]{0:T(256)S(1)} %bitcast.55, f32[256]{0:T(256)S(1)} %bitcast.49, f32[256]{0:T(256)S(1)} %bitcast.51, f32[256]{0:T(256)S(1)} %bitcast.52, ...), kind=kLoop, calls=%fused_computation.9 | loop fusion | flops 1966080 | bytes 3154944 | tf_op jit(solution)/shard_map/add | solution.py:371
  4.3 0.2 fusion
  4.4 5.7 %psum.7 = f32[3,256]{1,0:T(4,128)S(1)} all-reduce(f32[3,256]{1,0:T(4,128)S(1)} %fusion), channel_id=1, replica_groups=mesh['region'=4,'subj'=32] {'region'}, use_global_device_ids=true, to_apply=%region_1.0 | all-reduce | flops 768 | bytes 6144 | tf_op jit(solution)/shard_map/psum | solution.py:377
  10.2 0.2 subtract_convert_fusion.cent
  10.4 0.0 copy-start.1
  10.4 104.2 %gram.1 = (s16[32,256,256]{2,1,0:T(8,128)(2,1)}, bf16[32,2,16,128]{3,2,1,0:T(8,128)(2,1)S(1)}) custom-call(bf16[3,256,512]{2,1,0:T(8,128)(2,1)S(1)} %subtract_convert_fusion.cent, s32[8,512]{1,0:T(8,128)S(1)} %broadcast_in_dim.23.tgt), custom_call_target="tpu_custom_call" | custom-call | flops 12999999488 | bytes 10485760 | tf_op jit(solution)/shard_map/gram/pallas_call | solution.py:265
  114.6 0.0 copy-done.1
  114.6 0.0 copy-start
  114.7 2.2 %copy-done = s16[32,256,256]{2,1,0:T(8,128)(2,1)S(1)} copy-done((s16[32,256,256]{2,1,0:T(8,128)(2,1)S(1)}, s16[32,256,256]{2,1,0:T(8,128)(2,1)}, u32[]{:S(2)}) %copy-start) | copy-done | bytes 4194328
  116.8 15.5 %ordered.1 = f32[1,256,8192]{2,1,0:T(8,128)} custom-call(s32[8192]{0:T(1024)S(1)} %copy-done.1, s32[1]{0:T(128)} %bitcast.me, s16[32,256,256]{2,1,0:T(8,128)(2,1)S(1)} %copy-done, bf16[32,2,16,128]{3,2,1,0:T(8,128)(2,1)S(1)} %get-tuple-element.8.scale), custom_call_target="tpu_custom_call" | custom-call | bytes 12582912 | tf_op jit(solution)/shard_map/ordered/pallas_call | solution.py:344
  (2 shorter events, 0.0 us)
Async XLA Ops:
  10.4 104.3 %copy-start.1 = (s32[8192]{0:T(1024)S(1)}, s32[8192]{0:T(1024)}, u32[]{:S(2)}) copy-start(s32[8192]{0:T(1024)} %order.1) | copy-start | bytes 98308
  114.6 2.2 %copy-start = (s16[32,256,256]{2,1,0:T(8,128)(2,1)S(1)}, s16[32,256,256]{2,1,0:T(8,128)(2,1)}, u32[]{:S(2)}) copy-start(s16[32,256,256]{2,1,0:T(8,128)(2,1)} %get-tuple-element.7.q) | copy-start | bytes 12582916

commit v4 on v3

--- a/solution.py
+++ b/solution.py
@@ -20,7 +20,7 @@
     return (2 * l + c, 8 * lax.rem(y, 4) + 2 * lax.rem(z, 4) + u)
 
 
-def gram_kernel(cent, tgt, out, out_scale, snd, panels, scales, res, relay_ss, relay_rs, ring_ss, ring_rs, sib_ss, sib_rs, res_ss, res_rs, scale_ss, scale_rs):
+def gram_kernel(moved, part, labels, out, out_scale, cent, parts, snd, panels, scales, res, sum_ss, sum_rs, relay_ss, relay_rs, ring_ss, ring_rs, sib_ss, sib_rs, res_ss, res_rs, scale_ss, scale_rs):
     r, s = lax.axis_index("region"), lax.axis_index("subj")
     l, c = r // 2, lax.rem(r, 2)
     y, z, u = s // 8, lax.rem(s // 2, 4), lax.rem(s, 2)
@@ -40,7 +40,26 @@
             for uu in range(2):
                 pl.semaphore_signal(barrier, inc=1, device_id=dev(l, cc, y + k, z, uu), device_id_type=MESH)
                 pl.semaphore_signal(barrier, inc=1, device_id=dev(l, cc, y, z + k, uu), device_id_type=MESH)
+    lab = labels[...].astype(jnp.float32)[0:1, :]
+    n = lab.shape[1]
+    same = jnp.broadcast_to(lab, (128, n)).T[:, 0:1] == lab
+    before = lax.broadcasted_iota(jnp.int32, (n, n), 0) < lax.broadcasted_iota(jnp.int32, (n, n), 1)
+    rank = jnp.sum(jnp.where(jnp.logical_and(same, before), 1.0, 0.0), axis=0, keepdims=True)
+    row = (lab * CAP + rank).astype(jnp.int32)
     pl.semaphore_wait(barrier, 31)
+
+    def sums(k, owner):
+        return copy(part, parts.at[owner], sum_ss.at[k - 1], sum_rs.at[owner], (lax.rem(r + k, G), s))
+
+    for k in range(1, G):
+        sums(k, r).start()
+    parts[r] = part[...]
+    for k in range(1, G):
+        sums(k, lax.rem(r + k, G)).wait_recv()
+    mean = (parts[0] + parts[1] + parts[2] + parts[3]) * (1.0 / (G * moved.shape[2]))
+    for d in range(3):
+        column = jnp.broadcast_to(mean[d : d + 1], (128, B)).T
+        cent[d] = (moved[d] - jnp.concatenate([column] * (moved.shape[2] // 128), axis=1)).astype(jnp.bfloat16)
 
     def relay(half, region):
         lr, ur = region // 2, region % 2
@@ -48,15 +67,15 @@
         src, dst, rs = snd.at[half, region], panels.at[r, 0, half], relay_rs.at[half, r]
         return mine, src, dst, rs, copy(src, dst, relay_ss.at[half, region], rs, dev(lr, u, y, z, ur))
 
-    row = tgt[0:1, :]
     slots = lax.broadcasted_iota(jnp.int32, (CAP, row.shape[1]), 0)
     for half in range(2):
         for region in range(G):
             pick = jnp.where(slots + region * CAP == row, 1.0, 0.0).astype(jnp.bfloat16)
+            found = lax.dot_general(
+                cent[:, half * H : (half + 1) * H, :].reshape(3 * H, -1), pick, NT, preferred_element_type=jnp.float32
+            ).astype(jnp.bfloat16)
             for d in range(3):
-                snd[half, region, :, d * CAP : (d + 1) * CAP] = lax.dot_general(
-                    cent[d, half * H : (half + 1) * H, :], pick, NT, preferred_element_type=jnp.float32
-                ).astype(jnp.bfloat16)
+                snd[half, region, :, d * CAP : (d + 1) * CAP] = found[d * H : (d + 1) * H]
             mine, src, dst, rs, remote = relay(half, region)
 
             @pl.when(mine)
@@ -134,6 +153,7 @@
         ]
 
     blocks = {}
+    late = []
 
     def deliver(b, hb, a, a_halves, tiles):
         number = 8 * lax.rem(place(b)[0], 4) + 2 * lax.rem(place(b)[1], 4) + place(b)[2]
@@ -157,8 +177,16 @@
                 @pl.when(jnp.logical_not(own))
                 def _():
                     remote.start()
+            elif a == 1 or late is None:
+                remote.start()
             else:
-                remote.start()
+                across = place(a)[2] != u
+                pl.when(across)(remote.start)
+                late.append((jnp.logical_not(across), remote))
+
+    def release():
+        for there, remote in late:
+            pl.when(there)(remote.start)
 
     BOTH = (0, 1)
 
@@ -218,6 +246,9 @@
             share(3, half, g).start()
         for g in turn + [G]:
             send(5, 9, 10, half, g, zp).wait_recv()
+        if half == 1:
+            release()
+            late = None
         far = slice(0, 6), BOTH, slice(10, 11), here
         turned(products(*far), *far)
         got_share(3, half)
@@ -230,6 +261,8 @@
             tiles = straight(*opposite)
             turned([row[:1] for row in tiles], slice(6, 8), (1,), slice(10, 11), (0,))
 
+    for k in range(1, G):
+        sums(k, r).wait_send()
     for half in range(2):
         for region in range(G):
             mine, *_, remote = relay(half, region)
@@ -260,7 +293,7 @@
         copy(out_scale.at[b], out_scale.at[b], scale_ss.at[0], scale_rs.at[b], sibling).wait_recv()
 
 
-def gram(cent, tgt):
+def gram(moved, part, labels):
     dma = pltpu.SemaphoreType.DMA
     return pl.pallas_call(
         gram_kernel,
@@ -268,13 +301,17 @@
             jax.ShapeDtypeStruct((32, B, B), jnp.int16),
             jax.ShapeDtypeStruct((32, 2, 16, H), jnp.bfloat16),
         ),
-        in_specs=[pl.BlockSpec(memory_space=pltpu.VMEM)] * 2,
+        in_specs=[pl.BlockSpec(memory_space=pltpu.VMEM)] * 3,
         out_specs=[pl.BlockSpec(memory_space=pl.ANY)] * 2,
         scratch_shapes=[
+            pltpu.VMEM(moved.shape, jnp.bfloat16),
+            pltpu.VMEM((G, 8, B), jnp.float32),
             pltpu.VMEM((2, G, H, F), jnp.bfloat16),
             pltpu.VMEM((G, 11, 2, H, F), jnp.bfloat16),
             pltpu.VMEM((2, 11, 16, H), jnp.bfloat16),
             pltpu.VMEM((34, B, B), jnp.int16),
+            dma((G - 1,)),
+            dma((G,)),
             dma((2, G)),
             dma((2, G)),
             dma((6, 2, G + 1)),
@@ -291,7 +328,7 @@
         ),
         cost_estimate=pl.CostEstimate(flops=13 * 10**9, bytes_accessed=10 * 2**20, transcendentals=0),
         name="gram",
-    )(cent, tgt)
+    )(moved, part, labels)
 
 
 W = 1024
@@ -299,7 +336,7 @@
 U = 16
 
 
-def order_kernel(order, me, q, scale, out, table, even, odd):
+def order_kernel(order, me, q_hbm, scale, out, q, table, even, odd, sems):
     step = pl.program_id(0)
 
     @pl.when(step == 0)
@@ -318,7 +355,15 @@
                 table[pl.ds(b * 2 * B + i, B, stride=2), :] = values * column * row[:, lanes]
             return 0
 
-        lax.fori_loop(0, q.shape[0], decode, 0)
+        def fetch(k):
+            some = pl.ds(k * 4, 4)
+            return pltpu.make_async_copy(q_hbm.at[some], q.at[some], sems.at[k])
+
+        for k in range(8):
+            fetch(k).start()
+        for k in range(8):
+            fetch(k).wait()
+            lax.fori_loop(4 * k, 4 * k + 4, decode, 0)
 
     def gather(rows, t):
         for k in range(0, T, U):
@@ -348,24 +393,25 @@
             num_scalar_prefetch=2,
             grid=(n // W,),
             in_specs=[
-                pl.BlockSpec(q.shape, lambda i, o, m: (0, 0, 0), pipeline_mode=pl.Buffered(1)),
+                pl.BlockSpec(memory_space=pl.ANY),
                 pl.BlockSpec(scale.shape, lambda i, o, m: (0, 0, 0, 0), pipeline_mode=pl.Buffered(1)),
             ],
             out_specs=pl.BlockSpec((1, B, W), lambda i, o, m: (0, 0, i)),
             scratch_shapes=[
+                pltpu.VMEM(q.shape, q.dtype),
                 pltpu.VMEM((2 * n, 128), jnp.float32),
                 pltpu.VMEM((2 * T, 128), jnp.float32),
                 pltpu.VMEM((2 * T, 128), jnp.float32),
+                pltpu.SemaphoreType.DMA((8,)),
             ],
         ),
-        compiler_params=pltpu.CompilerParams(vmem_limit_bytes=40 * 2**20),
+        compiler_params=pltpu.CompilerParams(vmem_limit_bytes=58 * 2**20),
         cost_estimate=pl.CostEstimate(flops=0, bytes_accessed=6 * n * B, transcendentals=0),
         name="ordered",
     )(order, me, q, scale)
 
 
 def local(coords, transform, labels, subject_order):
-    verts = coords.shape[2] * lax.axis_size("region")
     moved = jnp.stack(
         [
             transform[:, d, 0:1] * coords[:, 0, :]
@@ -374,14 +420,9 @@
             for d in range(3)
         ]
     )
-    totals = lax.psum(jnp.sum(moved, axis=2), "region")
-    cent = (moved - (totals / verts)[:, :, None]).astype(jnp.bfloat16)
-    lab = labels[:, 0]
-    n = lab.shape[0]
-    before = jnp.arange(n)[:, None] < jnp.arange(n)[None, :]
-    rank = jnp.sum(jnp.where((labels == lab[None, :]) & before, 1, 0), axis=0)
-    tgt = jnp.broadcast_to((lab * CAP + rank)[None, :], (8, n))
-    return ordered(subject_order, lax.axis_index("subj")[None], *gram(cent, tgt))
+    part = jnp.pad(jnp.sum(moved, axis=2), ((0, 5), (0, 0)))
+    rows = jnp.broadcast_to(labels[:, 0][None, :], (8, labels.shape[0]))
+    return ordered(subject_order, lax.axis_index("subj")[None], *gram(moved, part, rows))
 
 
 def solution(mesh):

time: 133 us -> 128 us (0.962)
  blocking collectives: 5.73 us -> 0 us
  Pallas kernels: 120 us -> 123 us
  other arithmetic: 3.74 us -> 1.97 us
    psum x1 -> x0, blocking collectives: 5.73 us -> none  [local(): totals = lax.psum(jnp.sum(moved, axis=2), 'region')]
    pallas_call x1, Pallas kernels: 15.5 us -> 17.7 us  [ordered(): pl.pallas_call(order_kernel, out_shape=jax.ShapeDtypeStruct((1, B, n), jn...]
    unnamed x4 -> x2, local copies, waits for them, and re-layouts: 2.19 us -> 0.68 us
where the time goes in v4:
time: 128 us
  Pallas kernels  123 us (96%)
  local copies, waits for them, and re-layouts  2.23 us (2%)
  other arithmetic  1.97 us (2%)
    pallas_call x1, Pallas kernels, gram(): pl.pallas_call(gram_kernel, out_shape=(jax.ShapeDtypeStruct((32, B, B), j...  106 us
    pallas_call x1, Pallas kernels, ordered(): pl.pallas_call(order_kernel, out_shape=jax.ShapeDtypeStruct((1, B, n), jn...  17.7 us

profile of v4, /device:TPU:3, one launch (start us, length us, event | category | flops | bytes accessed | tf_op | source)
XLA Modules:
  0.0 127.6 jit_solution(10605319492393498859)
XLA Ops:
  0.0 0.9 fusion.7
  0.9 0.7 broadcast_in_dim.12.labels
  1.5 1.7 %fusion = (f32[1,256,512]{2,1,0:T(8,128)S(1)}, f32[1,256,512]{2,1,0:T(8,128)S(1)}, f32[1,256,512]{2,1,0:T(8,128)S(1)}) fusion(f32[256,3,512]{2,0,1:T(8,128)} %param.4, f32[256]{0:T(256)S(1)} %bitcast.52, f32[256]{0:T(256)S(1)} %bitcast.53, f32[256]{0:T(256)S(1)} %bitcast.47, f32[256]{0:T(256)S(1)} %bitcast.49, f32[256]{0:T(256)S(1)} %bitcast.50, ...), kind=kLoop, calls=%fused_computation.4 | loop fusion | flops 1966080 | bytes 3154944 | tf_op jit(solution)/shard_map/add | solution.py:417
  3.3 0.2 fusion.6
  3.5 105.5 %gram.1 = (s16[32,256,256]{2,1,0:T(8,128)(2,1)}, bf16[32,2,16,128]{3,2,1,0:T(8,128)(2,1)S(1)}) custom-call(f32[3,256,512]{2,1,0:T(8,128)S(1)} %get-tuple-element.10.moved, f32[8,256]{1,0:T(8,128)S(1)} %pad.4.part, s32[8,512]{1,0:T(8,128)S(1)} %broadcast_in_dim.12.labels), custom_call_target="tpu_custom_call" | custom-call | flops 12999999488 | bytes 10485760 | tf_op jit(solution)/shard_map/gram/pallas_call | solution.py:298
  109.1 0.0 copy-start
  109.1 0.7 copy-done
  109.8 17.7 %ordered.1 = f32[1,256,8192]{2,1,0:T(8,128)} custom-call(s32[8192]{0:T(1024)} %order.1, s32[1]{0:T(128)} %bitcast.me, s16[32,256,256]{2,1,0:T(8,128)(2,1)} %get-tuple-element.7.q_hbm, bf16[32,2,16,128]{3,2,1,0:T(8,128)(2,1)} %copy-done), custom_call_target="tpu_custom_call" | custom-call | bytes 12582912 | tf_op jit(solution)/shard_map/ordered/pallas_call | solution.py:389
  (1 shorter events, 0.0 us)
Async XLA Ops:
  109.1 0.7 copy-start

commit v5 on v4

--- a/solution.py
+++ b/solution.py
@@ -123,11 +123,11 @@
             x = panels[g, 0, half].astype(jnp.float32)
             square += jnp.sum(x * x, axis=1, keepdims=True)
         norm = jnp.broadcast_to(jnp.sqrt(square) * (1.0 + 2.0**-7), (H, 128)).T
-        scales[half, 0] = norm[0:16, :].astype(jnp.bfloat16)
+        scales[half, 0] = norm[0:1, :]
         send_own(half, G)
 
     def inverse(half, slot):
-        row = scales[half, slot].astype(jnp.float32)[0:1, :]
+        row = scales[half, slot]
         return jnp.where(row > 0.0, 1.0 / row, 0.0)
 
     def products(bs, b_halves, as_, a_halves):
@@ -160,9 +160,9 @@
         owner = dev(l, u, *place(a))
         t, b_halves = blocks.setdefault((b, a), (len(blocks), set()))
         b_halves.add(hb)
-        at = (pl.ds(hb * H, H), pl.ds(a_halves[0] * H, len(a_halves) * H))
+        at = (hb, pl.ds(a_halves[0], len(a_halves)))
         for ha, tile in zip(a_halves, tiles, strict=True):
-            res[t, hb * H : (hb + 1) * H, ha * H : (ha + 1) * H] = tile.astype(jnp.int32).astype(jnp.int16)
+            res[t, hb, ha] = tile.astype(jnp.int32).astype(jnp.int16)
         moves = [(res.at[(t, *at)], out.at[(number, *at)], res_ss.at[t], res_rs.at[number])]
         if 0 in a_halves:
             moves.append((scales.at[hb, b], out_scale.at[number, hb], scale_ss.at[t], scale_rs.at[number]))
@@ -277,11 +277,10 @@
             for pos in range(4):
                 share(pos, half, g).wait_send()
     for (_, a), (t, halves) in blocks.items():
-        part = pl.ds(min(halves) * H, len(halves) * H)
         some = pl.ds(min(halves), len(halves))
 
-        def left(t=t, part=part, some=some):
-            copy(res.at[t, part], out.at[0, part], res_ss.at[t], res_rs.at[0], sibling).wait_send()
+        def left(t=t, some=some):
+            copy(res.at[t, some], out.at[0, some], res_ss.at[t], res_rs.at[0], sibling).wait_send()
             copy(out_scale.at[0, some], out_scale.at[0, some], scale_ss.at[t], scale_rs.at[0], sibling).wait_send()
 
         if a == 0:
@@ -298,8 +297,8 @@
     return pl.pallas_call(
         gram_kernel,
         out_shape=(
-            jax.ShapeDtypeStruct((32, B, B), jnp.int16),
-            jax.ShapeDtypeStruct((32, 2, 16, H), jnp.bfloat16),
+            jax.ShapeDtypeStruct((32, 2, 2, H, H), jnp.int16),
+            jax.ShapeDtypeStruct((32, 2, 1, H), jnp.float32),
         ),
         in_specs=[pl.BlockSpec(memory_space=pltpu.VMEM)] * 3,
         out_specs=[pl.BlockSpec(memory_space=pl.ANY)] * 2,
@@ -308,8 +307,8 @@
             pltpu.VMEM((G, 8, B), jnp.float32),
             pltpu.VMEM((2, G, H, F), jnp.bfloat16),
             pltpu.VMEM((G, 11, 2, H, F), jnp.bfloat16),
-            pltpu.VMEM((2, 11, 16, H), jnp.bfloat16),
-            pltpu.VMEM((34, B, B), jnp.int16),
+            pltpu.VMEM((2, 11, 1, H), jnp.float32),
+            pltpu.VMEM((34, 2, 2, H, H), jnp.int16),
             dma((G - 1,)),
             dma((G,)),
             dma((2, G)),
@@ -341,18 +340,17 @@
 
     @pl.when(step == 0)
     def _():
-        def scale_row(b):
-            halves = [scale[b, half].astype(jnp.float32)[0:1, :] for half in range(2)]
-            return jnp.concatenate(halves, axis=1)
-
-        row = scale_row(me[0]) * (1.0 / (32767.0 * 3.0 * 2048.0))
+        def scale_row(b, half):
+            return scale[b, half]
+
+        row = [scale_row(me[0], half) * (1.0 / (32767.0 * 3.0 * 2048.0)) for half in range(2)]
 
         def decode(b, _):
-            column = jnp.broadcast_to(scale_row(b), (128, B)).T
-            for i in range(2):
-                lanes = slice(128 * i, 128 * (i + 1))
-                values = q[b, :, lanes].astype(jnp.int32).astype(jnp.float32)
-                table[pl.ds(b * 2 * B + i, B, stride=2), :] = values * column * row[:, lanes]
+            for hb in range(2):
+                column = jnp.broadcast_to(scale_row(b, hb), (128, H)).T
+                for ha in range(2):
+                    values = q[b, hb, ha].astype(jnp.int32).astype(jnp.float32)
+                    table[pl.ds(b * 2 * B + hb * 2 * H + ha, H, stride=2), :] = values * column * row[ha]
             return 0
 
         def fetch(k):

time: 128 us -> 126 us (0.984)
  Pallas kernels: 123 us -> 121 us
    pallas_call x1, Pallas kernels: 106 us -> 104 us  [gram(): pl.pallas_call(gram_kernel, out_shape=(jax.ShapeDtypeStruct((32, 2, 2, H,...]
where the time goes in v5:
time: 126 us; the launch traced here: 125 us
  Pallas kernels  121 us (96%)
  local copies, waits for them, and re-layouts  2.14 us (2%)
  other arithmetic  1.97 us (2%)
    pallas_call x1, Pallas kernels, gram(): pl.pallas_call(gram_kernel, out_shape=(jax.ShapeDtypeStruct((32, 2, 2, H,...  104 us
    pallas_call x1, Pallas kernels, ordered(): pl.pallas_call(order_kernel, out_shape=jax.ShapeDtypeStruct((1, B, n), jn...  17.4 us

profile of v5, /device:TPU:3, one launch (start us, length us, event | category | flops | bytes accessed | tf_op | source)
XLA Modules:
  0.0 125.5 jit_solution(11724030080408813638)
XLA Ops:
  0.0 0.9 fusion.7
  0.9 0.7 broadcast_in_dim.12.labels
  1.5 1.7 %fusion = (f32[1,256,512]{2,1,0:T(8,128)S(1)}, f32[1,256,512]{2,1,0:T(8,128)S(1)}, f32[1,256,512]{2,1,0:T(8,128)S(1)}) fusion(f32[256,3,512]{2,0,1:T(8,128)} %param.4, f32[256]{0:T(256)S(1)} %bitcast.52, f32[256]{0:T(256)S(1)} %bitcast.53, f32[256]{0:T(256)S(1)} %bitcast.47, f32[256]{0:T(256)S(1)} %bitcast.49, f32[256]{0:T(256)S(1)} %bitcast.50, ...), kind=kLoop, calls=%fused_computation.4 | loop fusion | flops 1966080 | bytes 3154944 | tf_op jit(solution)/shard_map/add | solution.py:415
  3.3 0.2 fusion.6
  3.5 103.7 %gram.1 = (s16[32,2,2,128,128]{4,3,2,1,0:T(8,128)(2,1)}, f32[32,2,1,128]{3,2,1,0:T(1,128)S(1)}) custom-call(f32[3,256,512]{2,1,0:T(8,128)S(1)} %get-tuple-element.10.moved, f32[8,256]{1,0:T(8,128)S(1)} %pad.4.part, s32[8,512]{1,0:T(8,128)S(1)} %broadcast_in_dim.12.labels), custom_call_target="tpu_custom_call" | custom-call | flops 12999999488 | bytes 10485760 | tf_op jit(solution)/shard_map/gram/pallas_call | solution.py:297
  107.3 0.0 copy-start
  107.3 0.6 copy-done
  107.9 17.4 %ordered.1 = f32[1,256,8192]{2,1,0:T(8,128)} custom-call(s32[8192]{0:T(1024)} %order.1, s32[1]{0:T(128)} %bitcast.me, s16[32,2,2,128,128]{4,3,2,1,0:T(8,128)(2,1)} %get-tuple-element.7.q_hbm, f32[32,2,1,128]{3,2,1,0:T(1,128)} %copy-done), custom_call_target="tpu_custom_call" | custom-call | bytes 12582912 | tf_op jit(solution)/shard_map/ordered/pallas_call | solution.py:387
  (1 shorter events, 0.0 us)
Async XLA Ops:
  107.3 0.6 copy-start

commit v6 on v5

--- a/solution.py
+++ b/solution.py
@@ -61,29 +61,31 @@
         column = jnp.broadcast_to(mean[d : d + 1], (128, B)).T
         cent[d] = (moved[d] - jnp.concatenate([column] * (moved.shape[2] // 128), axis=1)).astype(jnp.bfloat16)
 
-    def relay(half, region):
-        lr, ur = region // 2, region % 2
-        mine = jnp.logical_and(own, jnp.logical_and(l == lr, u == ur))
-        src, dst, rs = snd.at[half, region], panels.at[r, 0, half], relay_rs.at[half, r]
-        return mine, src, dst, rs, copy(src, dst, relay_ss.at[half, region], rs, dev(lr, u, y, z, ur))
+    def relay(half, i):
+        lr, ur = 1 - l if i in (1, 2) else l, 1 - u if i in (2, 3) else u
+        src, dst, rs = snd.at[half, i], panels.at[r, 0, half], relay_rs.at[half, r]
+        return 2 * lr + ur, src, dst, rs, copy(src, dst, relay_ss.at[half, i], rs, dev(lr, u, y, z, ur))
 
     slots = lax.broadcasted_iota(jnp.int32, (CAP, row.shape[1]), 0)
     for half in range(2):
-        for region in range(G):
+        for i in range(G):
+            region, src, dst, rs, remote = relay(half, i)
             pick = jnp.where(slots + region * CAP == row, 1.0, 0.0).astype(jnp.bfloat16)
             found = lax.dot_general(
                 cent[:, half * H : (half + 1) * H, :].reshape(3 * H, -1), pick, NT, preferred_element_type=jnp.float32
             ).astype(jnp.bfloat16)
             for d in range(3):
-                snd[half, region, :, d * CAP : (d + 1) * CAP] = found[d * H : (d + 1) * H]
-            mine, src, dst, rs, remote = relay(half, region)
-
-            @pl.when(mine)
-            def _():
-                pltpu.make_async_copy(src, dst, rs).start()
-
-            @pl.when(jnp.logical_not(mine))
-            def _():
+                snd[half, i, :, d * CAP : (d + 1) * CAP] = found[d * H : (d + 1) * H]
+            if i == 0:
+
+                @pl.when(own)
+                def _():
+                    pltpu.make_async_copy(src, dst, rs).start()
+
+                @pl.when(jnp.logical_not(own))
+                def _():
+                    remote.start()
+            else:
                 remote.start()
 
     sibling = dev(l, 1 - c, y, z, u)
@@ -264,11 +266,11 @@
     for k in range(1, G):
         sums(k, r).wait_send()
     for half in range(2):
-        for region in range(G):
-            mine, *_, remote = relay(half, region)
-
-            @pl.when(jnp.logical_not(mine))
-            def _():
+        for i in range(G):
+            *_, remote = relay(half, i)
+            if i == 0:
+                pl.when(jnp.logical_not(own))(remote.wait_send)
+            else:
                 remote.wait_send()
 
         for g in range(G + 1):

time: 126 us -> 125 us (level); the launches traced: 125 us -> 123 us
  Pallas kernels: 121 us -> 119 us
    pallas_call x1, Pallas kernels: 104 us -> 101 us  [gram(): pl.pallas_call(gram_kernel, out_shape=(jax.ShapeDtypeStruct((32, 2, 2, H,...]
where the time goes in v6:
time: 125 us; the launch traced here: 123 us
  Pallas kernels  119 us (95%)
  local copies, waits for them, and re-layouts  2.14 us (2%)
  other arithmetic  1.97 us (2%)
    pallas_call x1, Pallas kernels, gram(): pl.pallas_call(gram_kernel, out_shape=(jax.ShapeDtypeStruct((32, 2, 2, H,...  101 us
    pallas_call x1, Pallas kernels, ordered(): pl.pallas_call(order_kernel, out_shape=jax.ShapeDtypeStruct((1, B, n), jn...  17.4 us

profile of v6, /device:TPU:3, one launch (start us, length us, event | category | flops | bytes accessed | tf_op | source)
XLA Modules:
  0.0 123.2 jit_solution(17087475729205013664)
XLA Ops:
  0.0 0.9 fusion.7
  0.9 0.7 broadcast_in_dim.12.labels
  1.5 1.7 %fusion = (f32[1,256,512]{2,1,0:T(8,128)S(1)}, f32[1,256,512]{2,1,0:T(8,128)S(1)}, f32[1,256,512]{2,1,0:T(8,128)S(1)}) fusion(f32[256,3,512]{2,0,1:T(8,128)} %param.4, f32[256]{0:T(256)S(1)} %bitcast.52, f32[256]{0:T(256)S(1)} %bitcast.53, f32[256]{0:T(256)S(1)} %bitcast.47, f32[256]{0:T(256)S(1)} %bitcast.49, f32[256]{0:T(256)S(1)} %bitcast.50, ...), kind=kLoop, calls=%fused_computation.4 | loop fusion | flops 1966080 | bytes 3154944 | tf_op jit(solution)/shard_map/add | solution.py:417
  3.3 0.2 fusion.6
  3.5 101.4 %gram.1 = (s16[32,2,2,128,128]{4,3,2,1,0:T(8,128)(2,1)}, f32[32,2,1,128]{3,2,1,0:T(1,128)S(1)}) custom-call(f32[3,256,512]{2,1,0:T(8,128)S(1)} %get-tuple-element.10.moved, f32[8,256]{1,0:T(8,128)S(1)} %pad.4.part, s32[8,512]{1,0:T(8,128)S(1)} %broadcast_in_dim.12.labels), custom_call_target="tpu_custom_call" | custom-call | flops 12999999488 | bytes 10485760 | tf_op jit(solution)/shard_map/gram/pallas_call | solution.py:299
  105.0 0.0 copy-start
  105.0 0.6 copy-done
  105.6 17.4 %ordered.1 = f32[1,256,8192]{2,1,0:T(8,128)} custom-call(s32[8192]{0:T(1024)} %order.1, s32[1]{0:T(128)} %bitcast.me, s16[32,2,2,128,128]{4,3,2,1,0:T(8,128)(2,1)} %get-tuple-element.7.q_hbm, f32[32,2,1,128]{3,2,1,0:T(1,128)} %copy-done), custom_call_target="tpu_custom_call" | custom-call | bytes 12582912 | tf_op jit(solution)/shard_map/ordered/pallas_call | solution.py:389
  (1 shorter events, 0.0 us)
Async XLA Ops:
  105.0 0.6 copy-start
